TPU v7x, 256 devices: a whole 4x4x8 slice. The times are simulated.
256 devices in a mesh: batch: 4 (over x_lo, core), query: 64 (over y, z, x_hi).
Axes of the slice: x: 4 (x_hi: 2, x_lo: 2; x = x_hi * 2 + x_lo), y: 4, z: 8, core: 2. Of those that a mesh axis runs over, the one named last changes fastest.
Arguments:
- points: bfloat16 [4, 16384, 1024], P('batch', 'query'), may hold values from -100 to 100
- order: int32 [4, 64, 256], P('batch', 'query'), may hold values from 0 to 255, each once within a row
- cotangent: bfloat16 [4, 16384, 1024], P('batch', 'query'), may hold values from -6 to 6
- kv_cross: bfloat16 [4, 512, 2048], P('batch', 'query'), may hold values from -6 to 6
- self_qkv: bfloat16 [4, 512, 3072], P('batch', 'query'), may hold values from -400 to 400
- kv_weight: bfloat16 [1024, 2048], replicated, may hold values from -0.1875 to 0.1875
- out_weight: bfloat16 [1024, 1024], replicated, may hold values from -0.1875 to 0.1875
Outputs:
- grad_points: bfloat16 [4, 16384, 1024], P('batch', 'query')
- grad_latent: bfloat16 [4, 512, 1024], P('batch', 'query')
- grad_qkv: bfloat16 [4, 512, 3072], P('batch', 'query')
- grad_out_proj: float32 [1024, 1024], P('query')
Inputs may be any that keep to these rules, and one draw needn't show every extreme that they name: `order`: each row of 256 entries holds every number from 0 to 255 once.
All inputs are finite; a program needn't handle non-finite values.
Results may differ from a plain program's by a relative error of at most 0.015.
Values may be sent and summed in bfloat16 or wider, within the bound.
A program may use at most 128 MiB of HBM per device.

v0:
```python
import jax
import jax.numpy as jnp
from jax import lax
from jax.sharding import PartitionSpec as P

HEADS = 16


def inner(left, right):
    return lax.dot_general(
        left, right, (((1,), (1,)), ((), ())), preferred_element_type=jnp.float32
    )


def outer(left, right):
    return lax.dot_general(
        left, right, (((0,), (0,)), ((), ())), preferred_element_type=jnp.float32
    )


def project_exact(rows, weight_wide):
    return lax.dot_general(
        rows,
        weight_wide,
        (((1,), (1,)), ((), ())),
        precision=lax.Precision.HIGHEST,
        preferred_element_type=jnp.float32,
    )


def softmax_rows(scores):
    top = jnp.max(scores, axis=-1, keepdims=True)
    weights = jnp.exp(scores - top)
    return weights / jnp.sum(weights, axis=-1, keepdims=True)


def on_device(points, order, cotangent, kv_cross, self_qkv, kv_weight, out_weight):
    width = kv_weight.shape[0]
    head_size = width // HEADS
    rows_dev = points.shape[1]
    block = min(512, rows_dev)
    count = rows_dev // block
    scale = 1.0 / width**0.5
    sscale = 1.0 / head_size**0.5
    weight_wide = kv_weight.astype(jnp.float32)
    queries = points[0]
    grads_in = cotangent[0][order[0, 0]]
    cross_all, self_all = (
        lax.all_gather(kv_cross, "query", axis=1, tiled=True),
        lax.all_gather(self_qkv[:, :, width:], "query", axis=1, tiled=True),
    )
    keys = cross_all[0, :, :width]
    values = cross_all[0, :, width:]
    latents = keys.shape[0]
    owned = self_qkv.shape[1]
    query_blocks = queries.reshape(count, block, width)
    grad_blocks = grads_in.reshape(count, block, width)

    def cross_step(carry, items):
        qrows, grows = items
        probs = softmax_rows(inner(qrows, keys) * scale)
        dprob = inner(grows, values)
        delta = jnp.sum(probs * dprob, axis=-1, keepdims=True)
        dscore = (probs * (dprob - delta) * scale).astype(jnp.bfloat16)
        grad_rows = jnp.dot(dscore, keys, preferred_element_type=jnp.float32).astype(jnp.bfloat16)
        dkey = outer(dscore, qrows)
        dvalue = outer(probs.astype(jnp.bfloat16), grows)
        return ((carry[0] + dkey, carry[1] + dvalue), grad_rows)

    zero = jnp.zeros((latents, width), jnp.float32)
    (dkey_all, dvalue_all), grad_points = lax.scan(
        cross_step, (zero, zero), (query_blocks, grad_blocks)
    )
    terms = jnp.concatenate([dkey_all, dvalue_all], axis=1)
    summed = lax.psum_scatter(terms, "query", scatter_dimension=0, tiled=True)
    latent_grad = project_exact(summed, weight_wide).astype(jnp.bfloat16)
    q_own = self_qkv[0, :, :width].reshape(owned, HEADS, head_size)
    k_all = self_all[0, :, :width].reshape(latents, HEADS, head_size)
    v_all = self_all[0, :, width:].reshape(latents, HEADS, head_size)
    sprobs = softmax_rows(
        jnp.einsum("ihd,jhd->hij", q_own, k_all, preferred_element_type=jnp.float32) * sscale
    )
    sprobs_low = sprobs.astype(jnp.bfloat16)
    attended = jnp.einsum("hij,jhd->ihd", sprobs_low, v_all, preferred_element_type=jnp.float32)
    attended = attended.reshape(owned, width).astype(jnp.bfloat16)
    proj_term = outer(attended, latent_grad)
    proj_part = lax.psum_scatter(proj_term, "query", scatter_dimension=0, tiled=True)
    proj_grad = lax.psum(proj_part.astype(jnp.bfloat16), "batch").astype(jnp.float32)
    dattended = inner(latent_grad, out_weight).astype(jnp.bfloat16)
    dah = dattended.reshape(owned, HEADS, head_size)
    sdprob = jnp.einsum("ihd,jhd->hij", dah, v_all, preferred_element_type=jnp.float32)
    sdelta = jnp.sum(sprobs * sdprob, axis=-1, keepdims=True)
    sdscore = (sprobs * (sdprob - sdelta) * sscale).astype(jnp.bfloat16)
    dq_own = jnp.einsum("hij,jhd->ihd", sdscore, k_all, preferred_element_type=jnp.float32).reshape(
        owned, width
    )
    dk_all = jnp.einsum("hij,ihd->jhd", sdscore, q_own, preferred_element_type=jnp.float32).reshape(
        latents, width
    )
    dv_all = jnp.einsum(
        "hij,ihd->jhd", sprobs_low, dah, preferred_element_type=jnp.float32
    ).reshape(latents, width)
    dk_own, dv_own = (
        lax.psum_scatter(dk_all, "query", scatter_dimension=0, tiled=True),
        lax.psum_scatter(dv_all, "query", scatter_dimension=0, tiled=True),
    )
    grad_qkv = jnp.concatenate([dq_own, dk_own, dv_own], axis=1).astype(jnp.bfloat16)
    return (grad_points, latent_grad[None], grad_qkv[None], proj_grad)


def solution(mesh):
    placed = (
        P("batch", "query", None),
        P("batch", "query", None),
        P("batch", "query", None),
        P("batch", "query", None),
        P("batch", "query", None),
        P(),
        P(),
    )
    return jax.shard_map(
        on_device,
        mesh=mesh,
        in_specs=placed,
        out_specs=(
            P("batch", "query", None),
            P("batch", "query", None),
            P("batch", "query", None),
            P("query", None),
        ),
        check_vma=False,
    )
```

profile of v0, /device:TPU:1, one launch (start us, length us, event | category | flops | bytes accessed | tf_op | source)
XLA Modules:
  0.0 1735.9 jit_solution(14360416599799795550)
XLA Ops:
  7.2 0.0 copy-start
  7.2 0.0 all-gather.3.cloned.1.call-start
  7.2 0.7 all-gather.3.cloned.1.call-update
  7.9 0.0 all-gather.5.cloned.1.call-start
  8.0 1.4 slice.21
  9.3 0.0 all-gather.5.cloned.1.call-update
  9.4 0.0 reduce-scatter.5.cloned.1.call-start
  9.4 0.7 compare_select_fusion
  10.1 2.7 gather_fusion
  12.8 118.0 %all-gather.3.cloned.1.call-done = bf16[1,512,2048]{2,1,0:T(8,128)(2,1)} async-done(((bf16[1,8,2048]{2,1,0:T(8,128)(2,1)}), bf16[1,512,2048]{2,1,0:T(8,128)(2,1)}) %all-gather.3.cloned.1.call-update) | async-done | bytes 2097168 | tf_op jit(solution)/shard_map/all_gather | solution.py:49
  130.8 0.0 copy-start.4
  130.8 2.1 fusion.40
  132.9 0.2 fusion.21
  133.1 0.0 copy-done.4
  133.1 0.6 multiply_reduce_fusion
  133.7 0.0 copy-start.2
  133.7 0.0 copy-start.1
  133.7 0.6 fusion.22
  134.3 0.2 copy-done.2
  134.5 0.4 copy-done.1
  134.9 0.6 fusion.13
  135.6 2.4 pad_maximum_fusion
  138.0 0.0 slice-start
  138.0 0.0 reduce-scatter.5.cloned.1.call-update
  138.0 0.0 reduce-scatter.9.cloned.1.call-start
  138.1 0.6 slice-done
  138.7 0.1 reshape_squeeze.9
  138.8 111.6 %all-gather.5.cloned.1.call-done = bf16[1,512,2048]{2,1,0:T(8,128)(2,1)} async-done(((bf16[1,8,2048]{2,1,0:T(8,128)(2,1)}), bf16[1,512,2048]{2,1,0:T(8,128)(2,1)}) %all-gather.5.cloned.1.call-update) | async-done | bytes 2097168 | tf_op jit(solution)/shard_map/all_gather | solution.py:50
  250.4 3.1 fusion.39
  253.5 2.3 copy.17
  255.8 1.5 convolution_multiply_fusion.1
  257.3 2.7 fusion.41
  260.0 314.0 %reduce-scatter.5.cloned.1.call-done = f32[8,2048]{1,0:T(8,128)} async-done(((f32[512,2048]{1,0:T(8,128)}), f32[8,2048]{1,0:T(8,128)}) %reduce-scatter.5.cloned.1.call-update) | async-done | bytes 65552 | tf_op jit(solution)/shard_map/reduce_scatter | solution.py:75
  574.0 5.6 convolution_convert_fusion.4
  579.5 0.0 copy-done
  579.5 0.6 convolution_convert_fusion.3
  580.2 0.1 reshape.103
  580.3 1.9 fusion.27
  582.2 2.9 copy.25
  585.1 0.0 reduce-scatter.9.cloned.1.call-update
  585.2 0.0 reduce-scatter.7.cloned.1.call-start
  585.2 2.3 copy.19
  587.5 1.5 fusion.30
  589.0 2.2 fusion.12
  591.1 3.0 copy.23
  594.1 0.0 reduce-scatter.7.cloned.1.call-update
  594.1 0.0 reduce-scatter.11.cloned.1.call-start
  594.2 1.7 fusion.10
  595.9 0.1 convert_element_type.57
  596.0 0.0 copy-done.3
  596.0 2.7 fusion.42
  598.7 0.0 reduce-scatter.11.cloned.1.call-update
  598.7 2.7 fusion.2
  601.4 1.8 fusion.9
  603.2 0.1 concatenate.21
  603.3 338.1 %reduce-scatter.9.cloned.1.call-done = f32[8,1024]{1,0:T(8,128)} async-done(((f32[512,1024]{1,0:T(8,128)}), f32[8,1024]{1,0:T(8,128)}) %reduce-scatter.9.cloned.1.call-update) | async-done | bytes 32784 | tf_op jit(solution)/shard_map/reduce_scatter | solution.py:105
  941.4 0.8 convert_bitcast_fusion
  942.2 359.3 %reduce-scatter.7.cloned.1.call-done = f32[8,1024]{1,0:T(8,128)} async-done(((f32[512,1024]{1,0:T(8,128)}), f32[8,1024]{1,0:T(8,128)}) %reduce-scatter.7.cloned.1.call-update) | async-done | bytes 32784 | tf_op jit(solution)/shard_map/reduce_scatter | solution.py:104
  1301.5 0.8 convert_bitcast_fusion.1
  1302.3 0.6 pad_maximum_fusion.1
  1302.9 364.3 %reduce-scatter.11.cloned.1.call-done = f32[16,1024]{1,0:T(8,128)} async-done(((f32[1024,1024]{1,0:T(8,128)}), f32[16,1024]{1,0:T(8,128)}) %reduce-scatter.11.cloned.1.call-update) | async-done | bytes 65552 | tf_op jit(solution)/shard_map/reduce_scatter | solution.py:87
  1667.2 0.8 convert_element_type.58
  1668.0 60.3 %psum.7 = bf16[16,1024]{1,0:T(8,128)(2,1)S(1)} all-reduce(bf16[16,1024]{1,0:T(8,128)(2,1)S(1)} %convert_element_type.58), channel_id=1, replica_groups=mesh['batch'=4,'query'=64] {'batch'}, use_global_device_ids=true, to_apply=%region_10.11 | all-reduce | flops 16384 | bytes 65536 | tf_op jit(solution)/shard_map/psum | solution.py:88
  1728.4 0.6 convert_element_type.59
  (4 shorter events, 0.0 us)
Async XLA Ops:
  7.2 572.4 %copy-start = (bf16[1024,1024]{1,0:T(8,128)(2,1)S(1)}, bf16[1024,1024]{1,0:T(8,128)(2,1)}, u32[]{:S(2)}) copy-start(bf16[1024,1024]{1,0:T(8,128)(2,1)} %param.13) | copy-start | bytes 6291460
  7.2 123.6 %all-gather.3.cloned.1.call-start = ((), (), s32[]{:S(2)}) async-start(), calls=%async_computation.4 | async-start | bytes 2129920 | tf_op jit(solution)/shard_map/all_gather | solution.py:49
  7.9 242.5 %all-gather.5.cloned.1.call-start = ((), (), s32[]{:S(2)}) async-start(), calls=%async_computation.6 | async-start | bytes 2129920 | tf_op jit(solution)/shard_map/all_gather | solution.py:50
  9.4 564.6 %reduce-scatter.5.cloned.1.call-start = ((), (), s32[]{:S(2)}) async-start(), calls=%async_computation.5 | async-start | bytes 4259840 | tf_op jit(solution)/shard_map/reduce_scatter | solution.py:75
  130.8 2.3 copy-start.4
  133.7 0.8 copy-start.2
  133.7 1.2 copy-start.1
  138.0 0.7 slice-start
  138.0 803.4 %reduce-scatter.9.cloned.1.call-start = ((), (), s32[]{:S(2)}) async-start(), calls=%async_computation.8 | async-start | bytes 2129920 | tf_op jit(solution)/shard_map/reduce_scatter | solution.py:105
  579.5 16.5 copy-start.3
  585.2 716.4 %reduce-scatter.7.cloned.1.call-start = ((), (), s32[]{:S(2)}) async-start(), calls=%async_computation.7 | async-start | bytes 2129920 | tf_op jit(solution)/shard_map/reduce_scatter | solution.py:104
  594.1 1073.1 %reduce-scatter.11.cloned.1.call-start = ((), (), s32[]{:S(2)}) async-start(), calls=%async_computation.9 | async-start | bytes 4259840 | tf_op jit(solution)/shard_map/reduce_scatter | solution.py:87
Sparse Core Ops, SparseCore 0:
  11.6 119.1 all-gather.2
  134.9 115.3 all-gather.4
  252.9 320.9 reduce-scatter.4
  585.3 356.1 reduce-scatter.8
  943.8 357.7 reduce-scatter.6
  1304.1 363.0 reduce-scatter.10
where the time goes:
time: 1740 us
  waiting for transfers between devices  1610 us (93%)
  blocking collectives  60.3 us (3%)
  matrix products  26 us (1%)
  local copies, waits for them, and re-layouts  19.3 us (1%)
    reduce_scatter x1, waiting for transfers between devices, on_device(): lax.psum_scatter(proj_term, 'query', scatter_dimension=0, tiled=True)  364 us
    reduce_scatter x1, waiting for transfers between devices, on_device(): lax.psum_scatter(dk_all, 'query', scatter_dimension=0, tiled=True)  359 us
    reduce_scatter x1, waiting for transfers between devices, on_device(): lax.psum_scatter(dv_all, 'query', scatter_dimension=0, tiled=True)  338 us
    reduce_scatter x1, waiting for transfers between devices, on_device(): summed = lax.psum_scatter(terms, 'query', scatter_dimension=0, tiled=True)  314 us
    all_gather x1, waiting for transfers between devices, on_device(): lax.all_gather(kv_cross, 'query', axis=1, tiled=True)  118 us
    all_gather x1, waiting for transfers between devices, on_device(): lax.all_gather(self_qkv[:, :, width:], 'query', axis=1, tiled=True)  112 us
    psum x1, blocking collectives, on_device(): lax.psum(proj_part.astype(jnp.bfloat16), 'batch').astype(jnp.float32)  60.3 us
  transfers between devices with their start and end apart: 6, of which 6 were waited for; matrix products, arithmetic and copies ran while one was open for 2% of the time, Pallas kernels for 0%

commit v1 on v0

--- a/solution.py
+++ b/solution.py
@@ -47,7 +47,12 @@
     grads_in = cotangent[0][order[0, 0]]
     cross_all, self_all = (
         lax.all_gather(kv_cross, "query", axis=1, tiled=True),
-        lax.all_gather(self_qkv[:, :, width:], "query", axis=1, tiled=True),
+        jnp.concatenate(
+            lax.all_to_all(
+                jnp.stack([self_qkv[:, :, width:]] * lax.axis_size("query")), "query", 0, 0
+            ),
+            axis=1,
+        ),
     )
     keys = cross_all[0, :, :width]
     values = cross_all[0, :, width:]

time: 1740 us -> 1630 us (0.937)
  waiting for transfers between devices: 1610 us -> 1490 us
    all_gather x1 -> x0, waiting for transfers between devices: 112 us -> none  [on_device(): lax.all_gather(self_qkv[:, :, width:], 'query', axis=1, tiled=True)]
    reduce_scatter x1, waiting for transfers between devices: 314 us -> 257 us  [on_device(): summed = lax.psum_scatter(terms, 'query', scatter_dimension=0, tiled=True)]
    all_to_all x0 -> x1, waiting for transfers between devices: none -> 53.4 us  [on_device(): lax.all_to_all(jnp.stack([self_qkv[:, :, width:]] * lax.axis_size('query'...]
where the time goes in v1:
time: 1630 us
  waiting for transfers between devices  1490 us (91%)
  blocking collectives  60.6 us (4%)
  matrix products  25.9 us (2%)
  local copies, waits for them, and re-layouts  20.6 us (1%)
    reduce_scatter x1, waiting for transfers between devices, on_device(): lax.psum_scatter(proj_term, 'query', scatter_dimension=0, tiled=True)  365 us
    reduce_scatter x1, waiting for transfers between devices, on_device(): lax.psum_scatter(dk_all, 'query', scatter_dimension=0, tiled=True)  358 us
    reduce_scatter x1, waiting for transfers between devices, on_device(): lax.psum_scatter(dv_all, 'query', scatter_dimension=0, tiled=True)  337 us
    reduce_scatter x1, waiting for transfers between devices, on_device(): summed = lax.psum_scatter(terms, 'query', scatter_dimension=0, tiled=True)  257 us
    all_gather x1, waiting for transfers between devices, on_device(): lax.all_gather(kv_cross, 'query', axis=1, tiled=True)  119 us
    psum x1, blocking collectives, on_device(): lax.psum(proj_part.astype(jnp.bfloat16), 'batch').astype(jnp.float32)  60.6 us
    all_to_all x1, waiting for transfers between devices, on_device(): lax.all_to_all(jnp.stack([self_qkv[:, :, width:]] * lax.axis_size('query'...  53.4 us
  transfers between devices with their start and end apart: 6, of which 6 were waited for; matrix products, arithmetic and copies ran while one was open for 2% of the time, Pallas kernels for 0%

profile of v1, /device:TPU:1, one launch (start us, length us, event | category | flops | bytes accessed | tf_op | source)
XLA Modules:
  0.0 1629.3 jit_solution(18199625885150800180)
XLA Ops:
  7.2 0.0 copy-start
  7.2 0.0 all-gather.2.cloned.1.call-start
  7.2 0.7 all-gather.2.cloned.1.call-update
  7.9 0.0 reduce-scatter.5.cloned.1.call-start
  8.0 0.7 compare_select_fusion
  8.7 2.7 gather_fusion
  11.3 119.4 %all-gather.2.cloned.1.call-done = bf16[1,512,2048]{2,1,0:T(8,128)(2,1)} async-done(((bf16[1,8,2048]{2,1,0:T(8,128)(2,1)}), bf16[1,512,2048]{2,1,0:T(8,128)(2,1)}) %all-gather.2.cloned.1.call-update) | async-done | bytes 2097168 | tf_op jit(solution)/shard_map/all_gather | solution.py:49
  130.8 1.9 fusion.40
  132.7 0.0 copy-start.5
  132.7 0.2 fusion.21
  132.9 0.6 fusion.22
  133.6 0.7 copy-done.5
  134.3 0.0 copy-start.1
  134.3 0.6 multiply_reduce_fusion
  134.9 0.0 copy-start.2
  134.9 0.8 copy-done.2
  135.7 0.0 copy-done.1
  135.7 0.6 fusion.13
  136.3 2.4 pad_maximum_fusion
  138.8 0.0 reduce-scatter.5.cloned.1.call-update
  138.8 0.8 copy-done.4
  139.6 1.6 stack.2
  141.2 0.0 slice-start
  141.2 8.1 all-to-all-start
  149.3 0.0 reduce-scatter.9.cloned.1.call-start
  149.3 0.0 slice-done
  149.3 0.1 reshape_squeeze.9
  149.4 53.4 %all-to-all-done = bf16[64,1,8,2048]{3,2,1,0:T(8,128)(2,1)} async-done(((bf16[64,1,8,2048]{3,2,1,0:T(8,128)(2,1)}), bf16[64,1,8,2048]{3,2,1,0:T(8,128)(2,1)}, u32[]{:S(2)}, u32[]{:S(2)}) %all-to-all-start) | async-done | bytes 2097184 | tf_op jit(solution)/shard_map/all_to_all | solution.py:51
  202.8 3.1 fusion.39
  205.9 2.3 copy.26
  208.2 1.5 convolution_multiply_fusion.1
  209.6 2.7 fusion.41
  212.4 257.0 %reduce-scatter.5.cloned.1.call-done = f32[8,2048]{1,0:T(8,128)} async-done(((f32[512,2048]{1,0:T(8,128)}), f32[8,2048]{1,0:T(8,128)}) %reduce-scatter.5.cloned.1.call-update) | async-done | bytes 65552 | tf_op jit(solution)/shard_map/reduce_scatter | solution.py:80
  469.4 5.6 convolution_convert_fusion.4
  474.9 0.0 copy-done
  475.0 0.6 convolution_convert_fusion.3
  475.6 0.1 reshape.110
  475.7 1.9 fusion.27
  477.7 2.9 copy.34
  480.6 0.0 reduce-scatter.9.cloned.1.call-update
  480.6 0.0 reduce-scatter.7.cloned.1.call-start
  480.6 2.3 copy.28
  482.9 1.5 fusion.30
  484.4 2.2 fusion.12
  486.6 3.0 copy.32
  489.5 0.0 reduce-scatter.7.cloned.1.call-update
  489.6 0.0 reduce-scatter.11.cloned.1.call-start
  489.6 1.7 fusion.10
  491.3 0.1 convert_element_type.57
  491.4 0.0 copy-done.3
  491.4 2.7 fusion.42
  494.1 0.0 reduce-scatter.11.cloned.1.call-update
  494.1 2.7 fusion.2
  496.8 1.8 fusion.9
  498.7 0.1 concatenate.21
  498.8 336.9 %reduce-scatter.9.cloned.1.call-done = f32[8,1024]{1,0:T(8,128)} async-done(((f32[512,1024]{1,0:T(8,128)}), f32[8,1024]{1,0:T(8,128)}) %reduce-scatter.9.cloned.1.call-update) | async-done | bytes 32784 | tf_op jit(solution)/shard_map/reduce_scatter | solution.py:110
  835.7 0.8 convert_bitcast_fusion
  836.5 357.7 %reduce-scatter.7.cloned.1.call-done = f32[8,1024]{1,0:T(8,128)} async-done(((f32[512,1024]{1,0:T(8,128)}), f32[8,1024]{1,0:T(8,128)}) %reduce-scatter.7.cloned.1.call-update) | async-done | bytes 32784 | tf_op jit(solution)/shard_map/reduce_scatter | solution.py:109
  1194.1 0.8 convert_bitcast_fusion.1
  1194.9 0.6 pad_maximum_fusion.1
  1195.5 365.1 %reduce-scatter.11.cloned.1.call-done = f32[16,1024]{1,0:T(8,128)} async-done(((f32[1024,1024]{1,0:T(8,128)}), f32[16,1024]{1,0:T(8,128)}) %reduce-scatter.11.cloned.1.call-update) | async-done | bytes 65552 | tf_op jit(solution)/shard_map/reduce_scatter | solution.py:92
  1560.6 0.8 convert_element_type.58
  1561.5 60.6 %psum.7 = bf16[16,1024]{1,0:T(8,128)(2,1)S(1)} all-reduce(bf16[16,1024]{1,0:T(8,128)(2,1)S(1)} %convert_element_type.58), channel_id=1, replica_groups=mesh['batch'=4,'query'=64] {'batch'}, use_global_device_ids=true, to_apply=%region_10.11 | all-reduce | flops 16384 | bytes 65536 | tf_op jit(solution)/shard_map/psum | solution.py:93
  1622.1 0.6 convert_element_type.59
  (6 shorter events, 0.0 us)
Async XLA Ops:
  7.2 467.8 %copy-start = (bf16[1024,1024]{1,0:T(8,128)(2,1)S(1)}, bf16[1024,1024]{1,0:T(8,128)(2,1)}, u32[]{:S(2)}) copy-start(bf16[1024,1024]{1,0:T(8,128)(2,1)} %param.13) | copy-start | bytes 6291460
  7.2 123.6 %all-gather.2.cloned.1.call-start = ((), (), s32[]{:S(2)}) async-start(), calls=%async_computation.5 | async-start | bytes 2129920 | tf_op jit(solution)/shard_map/all_gather | solution.py:49
  7.9 461.5 %reduce-scatter.5.cloned.1.call-start = ((), (), s32[]{:S(2)}) async-start(), calls=%async_computation.6 | async-start | bytes 4259840 | tf_op jit(solution)/shard_map/reduce_scatter | solution.py:80
  132.7 1.6 copy-start.5
  134.3 1.4 copy-start.1
  134.9 0.8 copy-start.2
  138.8 0.8 copy-start.4
  141.2 8.1 slice-start
  141.2 61.6 %all-to-all-start = ((bf16[64,1,8,2048]{3,2,1,0:T(8,128)(2,1)}), bf16[64,1,8,2048]{3,2,1,0:T(8,128)(2,1)}, u32[]{:S(2)}, u32[]{:S(2)}) async-start(bf16[64,1,8,2048]{3,2,1,0:T(8,128)(2,1)} %stack.2), calls=%async_computation.1 | async-start | bytes 4194304 | tf_op jit(solution)/shard_map/all_to_all | solution.py:51
  149.3 686.4 %reduce-scatter.9.cloned.1.call-start = ((), (), s32[]{:S(2)}) async-start(), calls=%async_computation.8 | async-start | bytes 2129920 | tf_op jit(solution)/shard_map/reduce_scatter | solution.py:110
  474.9 16.5 %copy-start.3 = (bf16[8,1024]{1,0:T(8,128)(2,1)}, bf16[8,1024]{1,0:T(8,128)(2,1)S(1)}, u32[]{:S(2)}) copy-start(bf16[8,1024]{1,0:T(8,128)(2,1)S(1)} %convolution_convert_fusion.4) | copy-start | bytes 49156
  480.6 713.6 %reduce-scatter.7.cloned.1.call-start = ((), (), s32[]{:S(2)}) async-start(), calls=%async_computation.7 | async-start | bytes 2129920 | tf_op jit(solution)/shard_map/reduce_scatter | solution.py:109
  489.6 1071.1 %reduce-scatter.11.cloned.1.call-start = ((), (), s32[]{:S(2)}) async-start(), calls=%async_computation.9 | async-start | bytes 4259840 | tf_op jit(solution)/shard_map/reduce_scatter | solution.py:92
Sparse Core Ops, SparseCore 0:
  11.6 119.1 all-gather.1
  138.9 330.4 reduce-scatter.4
  480.7 354.9 reduce-scatter.8
  838.1 356.0 reduce-scatter.6
  1196.7 363.9 reduce-scatter.10
